TPU v7x, 32 devices: a whole 2x2x4 slice. The times are simulated.
32 devices in a mesh: row: 8 (over z, y), col: 4 (over x, core).
Axes of the slice: x: 2, y: 2, z: 4, core: 2. Of those that a mesh axis runs over, the one named last changes fastest.
Arguments:
- coords: float32 [4, 3, 8, 4096], P(None, None, None, ('row', 'col')), may hold values from -6 to 6
- chrom_lengths: int32 [46], replicated, may hold values from 1 to 2048, 32768 in all
- band_counts: int32 [4, 8, 32, 32], P(None, None, ('row', 'col')), may hold values from 16 to 111
- inter_pairs: int32 [4, 1024, 2], replicated, may hold values from 0 to 255, as said below
- inter_counts: int32 [4, 1024], replicated, may hold values from 16 to 111
Outputs:
- grad: float32 [4, 3, 8, 4096], P(None, None, None, ('row', 'col'))
Inputs may be any that keep to these rules, and one draw needn't show every extreme that they name: `inter_pairs`: every entry names two blocks of the structure. for every g in 0 to 7 and h in 0 to 3, at most 64 entries of one structure have (I mod 32) div 4 = g and J mod 4 = h, and one such (g, h) has exactly 64; the same holds with the roles of I and J exchanged.
All inputs are finite; a program needn't handle non-finite values.
Results may differ from a plain program's by a relative error of at most 0.0003.
Values sent between devices are 32-bit elements; how exact they have to be, the bound alone decides.
No kernel may reach another device: no remote copies, remote signals or barrier semaphores. Data moves between devices by JAX's collectives and lax.ppermute only.
A program may use at most 64 MiB of HBM per device.

v0:
```python
import jax
import jax.numpy as jnp
from jax import lax
from jax.sharding import PartitionSpec as P

LIST_CAP = 64


CONTACT_SHIFT = 3.0
CONTACT_SLOPE = 0.5
BACKGROUND = 0.5


def chromosome(beads, chrom_ends):
    return jnp.sum((chrom_ends <= beads[..., None]).astype(jnp.int32), axis=-1)


def pair_tiles(
    first_points,
    second_points,
    left_chrom,
    right_chrom,
    first_bead,
    second_bead,
    relation,
    tile_valid,
    tile_counts,
):
    block_size = first_points.shape[3]
    difference = first_points[:, :, :, :, None] - second_points[:, :, :, None, :]
    distance = jnp.sum(difference * difference, axis=1)
    chance = jax.nn.sigmoid(CONTACT_SHIFT - CONTACT_SLOPE * distance)
    same_chrom = left_chrom[:, :, :, None] == right_chrom[:, :, None, :]
    pair_order = jnp.sign(second_bead[:, :, None, :] - first_bead[:, :, :, None])
    wanted = relation[:, :, None, None]
    pair_mask = jnp.where(
        wanted == 0, jnp.logical_not(same_chrom), same_chrom & (pair_order == wanted)
    )
    masked = chance * (pair_mask.astype(jnp.float32) * tile_valid[:, :, None, None])
    expect = BACKGROUND + jnp.sum(masked, axis=(2, 3)) / block_size
    weight = 1.0 - tile_counts.astype(jnp.float32) / expect
    factor = (
        -2.0 * CONTACT_SLOPE / block_size * (masked * (1.0 - chance)) * weight[:, :, None, None]
    )
    pair_force = factor[:, None] * difference
    return (jnp.sum(pair_force, axis=4), -jnp.sum(pair_force, axis=3))


def on_device(coords, chrom_lengths, band_counts, inter_pairs, inter_counts):
    row_count = lax.axis_size("row")
    column_count = lax.axis_size("col")
    groups = row_count * column_count
    row_here = lax.axis_index("row")
    column_here = lax.axis_index("col")
    structures, _, sweeps, block_size = coords.shape
    band_reach = band_counts.shape[3] - 1
    column_steps = band_reach // column_count + 1
    chrom_ends = jnp.cumsum(chrom_lengths)
    beads_in = jnp.arange(block_size, dtype=jnp.int32)
    local_points = coords[:, :, None]
    local_counts = jnp.transpose(band_counts, (0, 2, 1, 3))
    row_points, row_counts = (
        lax.all_gather(local_points, "col", axis=2, tiled=True),
        lax.all_gather(local_counts, "col", axis=1, tiled=True),
    )
    column_points = lax.all_gather(local_points, "row", axis=2, tiled=True)
    row_flat = row_points.reshape(structures, 3, column_count * sweeps, block_size)
    column_flat = column_points.reshape(structures, 3, row_count * sweeps, block_size)
    column_slot = jnp.repeat(jnp.arange(column_count, dtype=jnp.int32), column_steps)
    step_slot = jnp.tile(jnp.arange(column_steps, dtype=jnp.int32), column_count)
    tile_total = column_slot.shape[0]
    up_gap = (column_here - column_slot) % column_count + step_slot * column_count
    up_pos = row_here * column_count + column_slot + up_gap
    up_shift = up_pos // groups
    up_row = up_pos % groups // column_count
    targets = jnp.arange(row_count * sweeps, dtype=jnp.int32)
    upward = jnp.ones((1, tile_total), jnp.int32)

    def sweep(column_total, sweep_turn):
        base_block = sweep_turn * groups + row_here * column_count + column_slot
        first_bead = base_block[:, None] * block_size + beads_in[None, :]
        left_chrom = chromosome(first_bead, chrom_ends)
        here_points = lax.dynamic_index_in_dim(row_points, sweep_turn, 3, keepdims=False)
        first_points = jnp.take(here_points, column_slot, axis=2)
        here_counts = lax.dynamic_index_in_dim(row_counts, sweep_turn, 2, keepdims=False)
        up_turn = sweep_turn + up_shift
        up_valid = (up_gap <= band_reach) & (up_turn < sweeps)
        up_index = up_row * sweeps + jnp.minimum(up_turn, sweeps - 1)
        second_points = jnp.take(column_flat, up_index, axis=2)
        second_bead = first_bead + up_gap[:, None] * block_size
        right_chrom = chromosome(second_bead, chrom_ends)
        tile_counts = here_counts[:, column_slot, jnp.minimum(up_gap, band_reach)]
        row_gain, column_gain = pair_tiles(
            first_points,
            second_points,
            left_chrom[None],
            right_chrom[None],
            first_bead[None],
            second_bead[None],
            upward,
            up_valid.astype(jnp.float32)[None],
            tile_counts,
        )
        rows_now = row_gain.reshape(structures, 3, column_count, column_steps, block_size).sum(3)
        placement = ((targets[None, :] == up_index[:, None]) & up_valid[:, None]).astype(
            jnp.float32
        )
        column_total = column_total + jnp.einsum(
            "sctb,tu->scub", column_gain, placement, precision=lax.Precision.HIGHEST
        )
        return (column_total, rows_now)

    column_total = jnp.zeros((structures, 3, row_count * sweeps, block_size), jnp.float32)
    column_total, rows_stack = lax.scan(sweep, column_total, jnp.arange(sweeps, dtype=jnp.int32))
    row_total = jnp.transpose(rows_stack, (1, 2, 3, 0, 4))
    first_blocks = inter_pairs[:, :, 0]
    second_blocks = inter_pairs[:, :, 1]
    entry_total = inter_pairs.shape[1]
    row_slots = jnp.arange(column_count * sweeps, dtype=jnp.int32)
    owned_tiles = (first_blocks % groups // column_count == row_here) & (
        second_blocks % column_count == column_here
    )
    entry_score = jnp.where(
        owned_tiles, entry_total - jnp.arange(entry_total, dtype=jnp.int32)[None, :], -1
    )
    top_score, picked = lax.top_k(entry_score, LIST_CAP)
    tile_valid = (top_score >= 0).astype(jnp.float32)
    first_block = jnp.take_along_axis(first_blocks, picked, axis=1)
    second_block = jnp.take_along_axis(second_blocks, picked, axis=1)
    tile_counts = jnp.take_along_axis(inter_counts, picked, axis=1)
    first_index = first_block % column_count * sweeps + first_block // groups
    second_index = second_block % groups // column_count * sweeps + second_block // groups
    first_points = jax.vmap(lambda points, indices: jnp.take(points, indices, axis=1))(
        row_flat, first_index
    )
    second_points = jax.vmap(lambda points, indices: jnp.take(points, indices, axis=1))(
        column_flat, second_index
    )
    first_bead = first_block[:, :, None] * block_size + beads_in
    second_bead = second_block[:, :, None] * block_size + beads_in
    row_gain, column_gain = pair_tiles(
        first_points,
        second_points,
        chromosome(first_bead, chrom_ends),
        chromosome(second_bead, chrom_ends),
        first_bead,
        second_bead,
        jnp.zeros_like(picked),
        tile_valid,
        tile_counts,
    )
    row_place = (row_slots[None, None, :] == first_index[:, :, None]).astype(jnp.float32)
    column_place = (targets[None, None, :] == second_index[:, :, None]).astype(jnp.float32)
    row_gain, column_gain, row_place, column_place = (
        row_gain,
        column_gain,
        row_place,
        column_place,
    )
    row_extra = jnp.einsum("sctb,stu->scub", row_gain, row_place, precision=lax.Precision.HIGHEST)
    column_total = column_total + jnp.einsum(
        "sctb,stu->scub", column_gain, column_place, precision=lax.Precision.HIGHEST
    )
    row_total = row_total + row_extra.reshape(structures, 3, column_count, sweeps, block_size)
    owned_rows = lax.psum_scatter(row_total, "col", scatter_dimension=2, tiled=True)
    result = owned_rows + lax.psum_scatter(
        column_total.reshape(structures, 3, row_count, sweeps, block_size),
        "row",
        scatter_dimension=2,
        tiled=True,
    )
    return result[:, :, 0]


def solution(mesh):
    placed = (
        P(None, None, None, ("row", "col")),
        P(),
        P(None, None, ("row", "col"), None),
        P(),
        P(),
    )
    return jax.shard_map(
        on_device,
        mesh=mesh,
        in_specs=placed,
        out_specs=P(None, None, None, ("row", "col")),
        check_vma=False,
    )
```

profile of v0, /device:TPU:0, one launch (start us, length us, event | category | flops | bytes accessed | tf_op | source)
XLA Modules:
  0.0 627.9 jit_solution(15012670291766712205)
XLA Ops:
  9.6 7.2 %all-gather = f32[4,3,32,128]{3,1,2,0:T(4,128)S(1)} all-gather(f32[4,3,8,128]{3,1,2,0:T(4,128)S(1)} %copy.50), channel_id=2, replica_groups=mesh['row'=8,'col'=4] {'col'}, dimensions={2}, use_global_device_ids=true | all-gather | bytes 245760 | tf_op jit(solution)/shard_map/all_gather | solution.py:63
  16.8 31.9 %all-gather.1 = f32[4,3,64,128]{3,1,2,0:T(4,128)S(1)} all-gather(f32[4,3,8,128]{3,1,2,0:T(4,128)S(1)} %copy.50), channel_id=3, replica_groups=mesh['row'=8,'col'=4] {'row'}, dimensions={2}, use_global_device_ids=true | all-gather | bytes 442368 | tf_op jit(solution)/shard_map/all_gather | solution.py:66
  49.7 5.5 all-gather.2
  55.5 385.3 %while.18 = (s32[]{:T(128)}, f32[4,3,64,128]{3,2,1,0:T(8,128)S(1)}, f32[8,4,3,4,128]{4,0,2,1,3:T(8,128)}, s32[8]{0:T(128)S(1)}, f32[4,3,4,8,128]{4,0,2,1,3:T(4,1...) while((s32[]{:T(128)}, f32[4,3,64,128]{3,2,1,0:T(8,128)S(1)}, ...), condition=%wide.region_9.10_spmd.clone.clone.clone.clone, body=%wide.region_1.9_spmd.clone.clone.clone.clone.sunk | while | flops 117820808 | bytes 53316460 | solution.py:114
  62.3 1.2 fusion.89
  63.5 11.6 %fusion.91 = f32[4,32,128,128]{3,2,1,0:T(8,128)} fusion(f32[4,3,32,128]{3,2,1,0:T(8,128)S(1)} %copy.88, f32[4,3,32,128]{3,2,1,0:T(8,128)S(1)} %copy.89), kind=kLoop, calls=%fused_computation.18.clone.1 | loop fusion | flops 16777216 | bytes 8781824 | tf_op jit(solution)/shard_map/while/body/eval_jaxpr/reduce_sum | solution.py:31
  75.1 5.4 multiply_reduce_fusion.2
  80.5 5.0 multiply_multiply_fusion.3
  85.6 15.9 %fusion.92 = (f32[4,3,32,128]{3,2,1,0:T(8,128)S(1)}, f32[4,3,32,128]{3,2,1,0:T(8,128)S(1)}) fusion(f32[4,32,128,128]{3,2,1,0:T(8,128)S(1)} %multiply_multiply_fusion.3, f32[4,3,32,128]{3,2,1,0:T(8,128)S(1)} %copy.88, f32[4,3,32,128]{3,2,1,0:T(8,128)S(1)} %copy.89), kind=kLoop, calls=%fused_computation.16.clone.1 | loop fusion | flops 25067520 | bytes 9175040 | tf_op jit(solution)/shard_map/while/body/eval_jaxpr/reduce_sum | solution.py:46
  101.5 1.7 dynamic_update_slice.11
  110.4 1.2 fusion.89
  111.6 11.6 %fusion.91 = f32[4,32,128,128]{3,2,1,0:T(8,128)} fusion(f32[4,3,32,128]{3,2,1,0:T(8,128)S(1)} %copy.88, f32[4,3,32,128]{3,2,1,0:T(8,128)S(1)} %copy.89), kind=kLoop, calls=%fused_computation.18.clone.1 | loop fusion | flops 16777216 | bytes 8781824 | tf_op jit(solution)/shard_map/while/body/eval_jaxpr/reduce_sum | solution.py:31
  123.2 5.4 multiply_reduce_fusion.2
  128.7 5.0 multiply_multiply_fusion.3
  133.7 15.9 %fusion.92 = (f32[4,3,32,128]{3,2,1,0:T(8,128)S(1)}, f32[4,3,32,128]{3,2,1,0:T(8,128)S(1)}) fusion(f32[4,32,128,128]{3,2,1,0:T(8,128)S(1)} %multiply_multiply_fusion.3, f32[4,3,32,128]{3,2,1,0:T(8,128)S(1)} %copy.88, f32[4,3,32,128]{3,2,1,0:T(8,128)S(1)} %copy.89), kind=kLoop, calls=%fused_computation.16.clone.1 | loop fusion | flops 25067520 | bytes 9175040 | tf_op jit(solution)/shard_map/while/body/eval_jaxpr/reduce_sum | solution.py:46
  149.7 1.7 dynamic_update_slice.11
  159.8 11.6 %fusion.91 = f32[4,32,128,128]{3,2,1,0:T(8,128)} fusion(f32[4,3,32,128]{3,2,1,0:T(8,128)S(1)} %copy.88, f32[4,3,32,128]{3,2,1,0:T(8,128)S(1)} %copy.89), kind=kLoop, calls=%fused_computation.18.clone.1 | loop fusion | flops 16777216 | bytes 8781824 | tf_op jit(solution)/shard_map/while/body/eval_jaxpr/reduce_sum | solution.py:31
  171.4 5.4 multiply_reduce_fusion.2
  176.8 5.0 multiply_multiply_fusion.3
  181.9 15.9 %fusion.92 = (f32[4,3,32,128]{3,2,1,0:T(8,128)S(1)}, f32[4,3,32,128]{3,2,1,0:T(8,128)S(1)}) fusion(f32[4,32,128,128]{3,2,1,0:T(8,128)S(1)} %multiply_multiply_fusion.3, f32[4,3,32,128]{3,2,1,0:T(8,128)S(1)} %copy.88, f32[4,3,32,128]{3,2,1,0:T(8,128)S(1)} %copy.89), kind=kLoop, calls=%fused_computation.16.clone.1 | loop fusion | flops 25067520 | bytes 9175040 | tf_op jit(solution)/shard_map/while/body/eval_jaxpr/reduce_sum | solution.py:46
  197.8 1.7 dynamic_update_slice.11
  206.7 1.2 fusion.89
  207.9 11.6 %fusion.91 = f32[4,32,128,128]{3,2,1,0:T(8,128)} fusion(f32[4,3,32,128]{3,2,1,0:T(8,128)S(1)} %copy.88, f32[4,3,32,128]{3,2,1,0:T(8,128)S(1)} %copy.89), kind=kLoop, calls=%fused_computation.18.clone.1 | loop fusion | flops 16777216 | bytes 8781824 | tf_op jit(solution)/shard_map/while/body/eval_jaxpr/reduce_sum | solution.py:31
  219.5 5.4 multiply_reduce_fusion.2
  225.0 5.0 multiply_multiply_fusion.3
  230.0 15.9 %fusion.92 = (f32[4,3,32,128]{3,2,1,0:T(8,128)S(1)}, f32[4,3,32,128]{3,2,1,0:T(8,128)S(1)}) fusion(f32[4,32,128,128]{3,2,1,0:T(8,128)S(1)} %multiply_multiply_fusion.3, f32[4,3,32,128]{3,2,1,0:T(8,128)S(1)} %copy.88, f32[4,3,32,128]{3,2,1,0:T(8,128)S(1)} %copy.89), kind=kLoop, calls=%fused_computation.16.clone.1 | loop fusion | flops 25067520 | bytes 9175040 | tf_op jit(solution)/shard_map/while/body/eval_jaxpr/reduce_sum | solution.py:46
  246.0 1.7 dynamic_update_slice.11
  254.9 1.2 fusion.89
  256.1 11.6 %fusion.91 = f32[4,32,128,128]{3,2,1,0:T(8,128)} fusion(f32[4,3,32,128]{3,2,1,0:T(8,128)S(1)} %copy.88, f32[4,3,32,128]{3,2,1,0:T(8,128)S(1)} %copy.89), kind=kLoop, calls=%fused_computation.18.clone.1 | loop fusion | flops 16777216 | bytes 8781824 | tf_op jit(solution)/shard_map/while/body/eval_jaxpr/reduce_sum | solution.py:31
  267.7 5.4 multiply_reduce_fusion.2
  273.1 5.0 multiply_multiply_fusion.3
  278.2 15.9 %fusion.92 = (f32[4,3,32,128]{3,2,1,0:T(8,128)S(1)}, f32[4,3,32,128]{3,2,1,0:T(8,128)S(1)}) fusion(f32[4,32,128,128]{3,2,1,0:T(8,128)S(1)} %multiply_multiply_fusion.3, f32[4,3,32,128]{3,2,1,0:T(8,128)S(1)} %copy.88, f32[4,3,32,128]{3,2,1,0:T(8,128)S(1)} %copy.89), kind=kLoop, calls=%fused_computation.16.clone.1 | loop fusion | flops 25067520 | bytes 9175040 | tf_op jit(solution)/shard_map/while/body/eval_jaxpr/reduce_sum | solution.py:46
  294.2 1.7 dynamic_update_slice.11
  303.0 1.2 fusion.89
  304.2 11.6 %fusion.91 = f32[4,32,128,128]{3,2,1,0:T(8,128)} fusion(f32[4,3,32,128]{3,2,1,0:T(8,128)S(1)} %copy.88, f32[4,3,32,128]{3,2,1,0:T(8,128)S(1)} %copy.89), kind=kLoop, calls=%fused_computation.18.clone.1 | loop fusion | flops 16777216 | bytes 8781824 | tf_op jit(solution)/shard_map/while/body/eval_jaxpr/reduce_sum | solution.py:31
  315.8 5.4 multiply_reduce_fusion.2
  321.3 5.0 multiply_multiply_fusion.3
  326.3 15.9 %fusion.92 = (f32[4,3,32,128]{3,2,1,0:T(8,128)S(1)}, f32[4,3,32,128]{3,2,1,0:T(8,128)S(1)}) fusion(f32[4,32,128,128]{3,2,1,0:T(8,128)S(1)} %multiply_multiply_fusion.3, f32[4,3,32,128]{3,2,1,0:T(8,128)S(1)} %copy.88, f32[4,3,32,128]{3,2,1,0:T(8,128)S(1)} %copy.89), kind=kLoop, calls=%fused_computation.16.clone.1 | loop fusion | flops 25067520 | bytes 9175040 | tf_op jit(solution)/shard_map/while/body/eval_jaxpr/reduce_sum | solution.py:46
  342.3 1.7 dynamic_update_slice.11
  351.2 1.2 fusion.89
  352.4 11.6 %fusion.91 = f32[4,32,128,128]{3,2,1,0:T(8,128)} fusion(f32[4,3,32,128]{3,2,1,0:T(8,128)S(1)} %copy.88, f32[4,3,32,128]{3,2,1,0:T(8,128)S(1)} %copy.89), kind=kLoop, calls=%fused_computation.18.clone.1 | loop fusion | flops 16777216 | bytes 8781824 | tf_op jit(solution)/shard_map/while/body/eval_jaxpr/reduce_sum | solution.py:31
  364.0 5.4 multiply_reduce_fusion.2
  369.5 5.0 multiply_multiply_fusion.3
  374.5 15.9 %fusion.92 = (f32[4,3,32,128]{3,2,1,0:T(8,128)S(1)}, f32[4,3,32,128]{3,2,1,0:T(8,128)S(1)}) fusion(f32[4,32,128,128]{3,2,1,0:T(8,128)S(1)} %multiply_multiply_fusion.3, f32[4,3,32,128]{3,2,1,0:T(8,128)S(1)} %copy.88, f32[4,3,32,128]{3,2,1,0:T(8,128)S(1)} %copy.89), kind=kLoop, calls=%fused_computation.16.clone.1 | loop fusion | flops 25067520 | bytes 9175040 | tf_op jit(solution)/shard_map/while/body/eval_jaxpr/reduce_sum | solution.py:46
  390.5 1.7 dynamic_update_slice.11
  400.6 11.6 %fusion.91 = f32[4,32,128,128]{3,2,1,0:T(8,128)} fusion(f32[4,3,32,128]{3,2,1,0:T(8,128)S(1)} %copy.88, f32[4,3,32,128]{3,2,1,0:T(8,128)S(1)} %copy.89), kind=kLoop, calls=%fused_computation.18.clone.1 | loop fusion | flops 16777216 | bytes 8781824 | tf_op jit(solution)/shard_map/while/body/eval_jaxpr/reduce_sum | solution.py:31
  412.2 5.4 multiply_reduce_fusion.2
  417.6 5.0 multiply_multiply_fusion.3
  422.6 15.9 %fusion.92 = (f32[4,3,32,128]{3,2,1,0:T(8,128)S(1)}, f32[4,3,32,128]{3,2,1,0:T(8,128)S(1)}) fusion(f32[4,32,128,128]{3,2,1,0:T(8,128)S(1)} %multiply_multiply_fusion.3, f32[4,3,32,128]{3,2,1,0:T(8,128)S(1)} %copy.88, f32[4,3,32,128]{3,2,1,0:T(8,128)S(1)} %copy.89), kind=kLoop, calls=%fused_computation.16.clone.1 | loop fusion | flops 25067520 | bytes 9175040 | tf_op jit(solution)/shard_map/while/body/eval_jaxpr/reduce_sum | solution.py:46
  438.6 1.7 dynamic_update_slice.11
  441.6 2.5 gather_fusion.6
  444.1 2.5 gather_fusion.5
  448.2 2.7 gather_fusion.7
  451.3 1.3 gather_fusion.4
  453.0 1.3 gather_fusion.3
  454.7 1.2 convert_reduce_fusion.3
  455.9 22.3 %fusion.37 = f32[4,64,128,128]{3,2,1,0:T(8,128)} fusion(f32[4,3,64,128]{3,2,1,0:T(8,128)S(1)} %copy.60, f32[4,3,64,128]{3,2,1,0:T(8,128)S(1)} %copy.59), kind=kLoop, calls=%fused_computation.85 | loop fusion | flops 33554432 | bytes 17563648 | tf_op jit(solution)/shard_map/reduce_sum | solution.py:31
  478.3 10.6 %fusion.38 = f32[4,64]{1,0:T(4,128)S(1)} fusion(f32[4,64]{1,0:T(4,128)S(1)} %fusion.66, s32[4,64,128]{2,1,0:T(8,128)S(1)} %get-tuple-element.386, s32[4,64,128]{2,1,0:T(8,128)S(1)} %get-tuple-element.385, f32[4,64,128,128]{3,2,1,0:T(8,128)} %fusion.37), kind=kLoop, calls=%fused_computation.88 | loop fusion | flops 37748480 | bytes 17041408 | tf_op jit(solution)/shard_map/reduce_sum | solution.py:40
  489.5 10.3 %multiply_multiply_fusion.1 = f32[4,64,128,128]{3,2,1,0:T(8,128)S(1)} fusion(f32[4,64]{1,0:T(4,128)} %subtract_multiply_fusion.5, f32[4,64]{1,0:T(4,128)S(1)} %fusion.66, s32[4,64,128]{2,1,0:T(8,128)} %copy-done.5, s32[4,64,128]{2,1,0:T(8,128)S(1)} %get-tuple-element.385, f32[4,64,128,128]{3,2,1,0:T(8,128)S(1)} %copy-done.1), kind=kLoop, calls=%fused_computation.86 | loop fusion | flops 46137344 | bytes 33818624 | tf_op jit(solution)/shard_map/mul | solution.py:43
  499.8 33.4 %fusion.35 = (f32[4,3,64,128]{3,2,1,0:T(8,128)}, f32[4,3,64,128]{3,2,1,0:T(8,128)S(1)}) fusion(f32[4,64,128,128]{3,2,1,0:T(8,128)S(1)} %multiply_multiply_fusion.1, f32[4,3,64,128]{3,2,1,0:T(8,128)} %copy-done.3, f32[4,3,64,128]{3,2,1,0:T(8,128)} %copy-done.4), kind=kLoop, calls=%fused_computation.83 | loop fusion | flops 50135040 | bytes 18350080 | tf_op jit(solution)/shard_map/reduce_sum | solution.py:46
  534.3 1.5 fusion.40
  536.5 18.3 %reduce-scatter.3.cloned.1.call-done = f32[4,3,1,8,128]{4,3,1,0,2:T(8,128)} async-done(((f32[4,3,4,8,128]{4,3,1,0,2:T(8,128)}), f32[4,3,1,8,128]{4,3,1,0,2:T(8,128)}) %reduce-scatter.3.cloned.1.call-update) | async-done | bytes 49168 | tf_op jit(solution)/shard_map/reduce_scatter | solution.py:165
  554.9 65.0 %reduce-scatter.5.cloned.1.call-done = f32[4,3,1,8,128]{4,3,1,0,2:T(8,128)} async-done(((f32[4,3,8,8,128]{4,3,1,0,2:T(8,128)}), f32[4,3,1,8,128]{4,3,1,0,2:T(8,128)}) %reduce-scatter.5.cloned.1.call-update) | async-done | bytes 49168 | tf_op jit(solution)/shard_map/reduce_scatter | solution.py:166
  619.9 1.4 add_bitcast_fusion
  (312 shorter events, 51.7 us)
Async XLA Ops:
  6.5 441.6 %copy-start = (s32[4,1024]{1,0:T(4,128)S(1)}, s32[4,1024]{1,0:T(4,128)}, u32[]{:S(2)}) copy-start(s32[4,1024]{1,0:T(4,128)} %param.13) | copy-start | bytes 49156
  6.5 434.3 %top_k.31.cloned.1.call-start = ((), (), s32[]{:S(2)}) async-start(), calls=%async_computation.4 | async-start | bytes 98336 | tf_op jit(solution)/shard_map/top_k | solution.py:126
  8.7 546.2 %reduce-scatter.3.cloned.1.call-start = ((), (), s32[]{:S(2)}) async-start(), calls=%async_computation.2 | async-start | bytes 245760 | tf_op jit(solution)/shard_map/reduce_scatter | solution.py:165
  440.8 48.1 %copy-start.2 = (f32[4,3,64,128]{3,2,1,0:T(8,128)}, f32[4,3,64,128]{3,2,1,0:T(8,128)S(1)}, u32[]{:S(2)}) copy-start(f32[4,3,64,128]{3,2,1,0:T(8,128)S(1)} %get-tuple-element.194) | copy-start | bytes 1179652
  447.5 41.4 %copy-start.7 = (s32[4,64]{1,0:T(4,128)}, s32[4,64]{1,0:T(4,128)S(1)}, u32[]{:S(2)}) copy-start(s32[4,64]{1,0:T(4,128)S(1)} %get-tuple-element.418) | copy-start | bytes 3076
  453.0 35.9 %copy-start.3 = (f32[4,3,64,128]{3,2,1,0:T(8,128)}, f32[4,3,64,128]{3,2,1,0:T(8,128)S(1)}, u32[]{:S(2)}) copy-start(f32[4,3,64,128]{3,2,1,0:T(8,128)S(1)} %copy.60) | copy-start | bytes 1179652
  454.7 34.2 %copy-start.4 = (f32[4,3,64,128]{3,2,1,0:T(8,128)}, f32[4,3,64,128]{3,2,1,0:T(8,128)S(1)}, u32[]{:S(2)}) copy-start(f32[4,3,64,128]{3,2,1,0:T(8,128)S(1)} %copy.59) | copy-start | bytes 1179652
  455.9 33.0 %copy-start.5 = (s32[4,64,128]{2,1,0:T(8,128)}, s32[4,64,128]{2,1,0:T(8,128)S(1)}, u32[]{:S(2)}) copy-start(s32[4,64,128]{2,1,0:T(8,128)S(1)} %get-tuple-element.386) | copy-start | bytes 393220
  478.3 11.2 %copy-start.1 = (f32[4,64,128,128]{3,2,1,0:T(8,128)S(1)}, f32[4,64,128,128]{3,2,1,0:T(8,128)}, u32[]{:S(2)}) copy-start(f32[4,64,128,128]{3,2,1,0:T(8,128)} %fusion.37) | copy-start | bytes 50331652
  499.8 33.7 %copy-start.6 = (f32[8,4,3,4,128]{4,0,2,1,3:T(8,128)S(1)}, f32[8,4,3,4,128]{4,0,2,1,3:T(8,128)}, u32[]{:S(2)}) copy-start(f32[8,4,3,4,128]{4,0,2,1,3:T(8,128)} %get-tuple-element.191) | copy-start | bytes 589828
  499.8 34.5 %copy-start.8 = (s32[4,64]{1,0:T(4,128)S(1)}, s32[4,64]{1,0:T(4,128)}, u32[]{:S(2)}) copy-start(s32[4,64]{1,0:T(4,128)} %copy-done.7) | copy-start | bytes 3076
  534.2 85.7 %reduce-scatter.5.cloned.1.call-start = ((), (), s32[]{:S(2)}) async-start(), calls=%async_computation.3 | async-start | bytes 442368 | tf_op jit(solution)/shard_map/reduce_scatter | solution.py:166
Sparse Core Ops, SparseCore 0:
  9.8 3.3 top_k.33.cloned.1.call-done
  534.3 20.4 reduce-scatter.2
  558.5 61.3 reduce-scatter.4
  (1 shorter events, 0.0 us)
where the time goes:
time: 629 us; the launch traced here: 628 us
  other arithmetic  407 us (65%)
  waiting for transfers between devices  83.4 us (13%)
  local copies, waits for them, and re-layouts  54.1 us (9%)
  blocking collectives  44.6 us (7%)
  loops' own time  19.8 us (3%)
  between operations  13.4 us (2%)
    reduce_sum x9, other arithmetic, pair_tiles(): return (jnp.sum(pair_force, axis=4), -jnp.sum(pair_force, axis=3))  160 us
    reduce_sum x9, other arithmetic, pair_tiles(): distance = jnp.sum(difference * difference, axis=1)  115 us
    reduce_scatter x1, waiting for transfers between devices, on_device(): lax.psum_scatter(column_total.reshape(structures, 3, row_count, sweeps, b...  65 us
    reduce_sum x9, other arithmetic, pair_tiles(): expect = BACKGROUND + jnp.sum(masked, axis=(2, 3)) / block_size  54.2 us
    mul x18, other arithmetic, pair_tiles(): -2.0 * CONTACT_SLOPE / block_size * (masked * (1.0 - chance))  51.2 us
    all_gather x1, blocking collectives, on_device(): column_points = lax.all_gather(local_points, 'row', axis=2, tiled=True)  31.9 us
    another operation x1, loops' own time, on_device(): lax.scan(sweep, column_total, jnp.arange(sweeps, dtype=jnp.int32))  19.8 us
    reduce_scatter x1, waiting for transfers between devices, on_device(): lax.psum_scatter(row_total, 'col', scatter_dimension=2, tiled=True)  18.3 us
  transfers between devices with their start and end apart: 2, of which 2 were waited for; matrix products, arithmetic and copies ran while one was open for 0% of the time, Pallas kernels for 0%

commit v1 on v0

v1 whole, which is shorter than its diff:
```python
import functools

import jax
import jax.numpy as jnp
from jax import lax
from jax.experimental import pallas as pl
from jax.experimental.pallas import tpu as pltpu
from jax.sharding import PartitionSpec as P

CONTACT_SHIFT = 3.0
CONTACT_SLOPE = 0.5
BACKGROUND = 0.5
FAR = 32.0
UNIT = 8
POINT_ROWS = 16
VMEM = pl.BlockSpec(memory_space=pltpu.VMEM)
SMEM = pl.BlockSpec(memory_space=pltpu.SMEM)


def split(value):
    high = value.astype(jnp.bfloat16).astype(jnp.float32)
    return high, (value - high).astype(jnp.bfloat16).astype(jnp.float32)


def pack_kernel(n_col, coords_ref, counts_ref, *out_refs):
    structures = coords_ref.shape[0]
    width = counts_ref.shape[3]
    column_here = lax.axis_index("col")
    for k, out_ref in enumerate(out_refs):
        member = lax.rem(lax.rem(column_here + k, n_col), structures)
        out_ref[0:3] = coords_ref[member]
        out_ref[3] = jnp.zeros(out_ref.shape[1:], jnp.float32)
        out_ref[3, :, 0:width] = counts_ref[member][:, 0, :].astype(jnp.float32)


def list_kernel(sizes, reach_ref, pairs_ref, code_ref, place_ref, number_ref):
    n_row, n_col, structures, sweeps = sizes
    groups = n_row * n_col
    blocks = groups * sweeps
    slots = structures * sweeps
    family = lax.axis_index("row") * (n_col // structures) + lax.axis_index("col") // structures
    base = family * structures

    def at(block):
        return lax.rem(block, groups) * sweeps + lax.div(block, groups)

    def idle(position, carry):
        code_ref[position] = slots * (1 << 19)
        place_ref[position] = 0
        return carry

    lax.fori_loop(0, UNIT, idle, 0)

    def band(slot, number):
        block = lax.rem(slot, sweeps) * groups + base + lax.div(slot, sweeps)
        low = reach_ref[0, slot]
        high = reach_ref[1, slot]

        def add(other, number):
            first = jnp.minimum(block, other)
            code_ref[number] = at(other) + slot * (1 << 12) + slot * (1 << 19)
            place_ref[number] = at(first) * 128 + jnp.abs(block - other)
            return number + 1

        return lax.fori_loop(low, high + 1, add, number)

    number = lax.fori_loop(0, slots, band, jnp.int32(UNIT))

    def listed(step, number):
        for inner in range(8):
            entry = step * 8 + inner
            first = pairs_ref[0, entry]
            second = pairs_ref[1, entry]
            for block, other in ((first, second), (second, first)):
                slot = lax.rem(block, structures) * sweeps + lax.div(block, groups)
                code_ref[number] = at(other) + (slots + slot) * (1 << 12) + slot * (1 << 19)
                place_ref[number] = blocks * 128 + entry
                mine = lax.div(lax.rem(block, groups), structures) == family
                number = number + mine.astype(jnp.int32)
        return number

    number = lax.fori_loop(0, pairs_ref.shape[1] // 8, listed, number)
    lax.fori_loop(number, number + 2 * UNIT, idle, 0)
    number_ref[0] = lax.div(number - 1, UNIT)


def tile_kernel(
    sizes,
    code_ref,
    place_ref,
    number_ref,
    starts_ref,
    ends_ref,
    listed_ref,
    *refs,
):
    n_row, n_col, structures, sweeps = sizes
    groups = n_row * n_col
    blocks = groups * sweeps
    slots = structures * sweeps
    piece_refs = refs[:n_row]
    out_refs = refs[n_row : n_row + structures]
    second_ref, first_ref, counts_ref, rows_ref, own_ref, held_ref, sums_ref, picks_ref, diag_ref, total_ref = refs[
        n_row + structures :
    ]
    labels = starts_ref.shape[0]
    depth = 2 * POINT_ROWS + labels
    row_here = lax.axis_index("row")
    column_here = lax.axis_index("col")
    share = lax.div(column_here, structures)
    place_here = lax.rem(column_here, structures)
    lane = lax.broadcasted_iota(jnp.int32, (1, 128), 1)

    def member(block):
        bead = block * 128 + lane
        inside = (bead >= starts_ref[...]) & (bead < ends_ref[...])
        return inside.astype(jnp.float32)

    def points(piece_ref, turn):
        parts = [split(piece_ref[turn, k]) for k in range(3)]
        near = [high + low for high, low in parts]
        norm = -0.5 * CONTACT_SLOPE * (near[0] * near[0] + near[1] * near[1] + near[2] * near[2])
        return parts, norm

    row = lax.broadcasted_iota(jnp.int32, (POINT_ROWS, 128), 0)
    fixed = jnp.where((row == 4) | (row == 5), 1.0, 0.0)
    for u in range(sweeps):
        rows_ref[u * POINT_ROWS : (u + 1) * POINT_ROWS] = fixed
    for k in range(n_row):
        origin = lax.rem(row_here + (n_row - k), n_row)

        def prepare(turn, carry, k=k, origin=origin):
            column = lax.rem(column_here + (n_col - turn), n_col)
            group = origin * n_col + column
            parts, norm = points(piece_refs[k], turn)
            for place, (high, low) in enumerate(parts + [split(norm)]):
                rows_ref[pl.ds(place, sweeps, stride=POINT_ROWS), :] = high
                rows_ref[pl.ds(place + 8, sweeps, stride=POINT_ROWS), :] = low
            counts_ref[pl.ds(pl.multiple_of(group * sweeps, sweeps), sweeps), :] = piece_refs[k][turn, 3]
            for u in range(sweeps):
                features = rows_ref[u * POINT_ROWS : (u + 1) * POINT_ROWS].astype(jnp.bfloat16)
                at = group * sweeps + u
                second_ref[at, 0:POINT_ROWS] = features
                second_ref[at, POINT_ROWS : 2 * POINT_ROWS] = features
                second_ref[at, 2 * POINT_ROWS : depth] = member(u * groups + group).astype(jnp.bfloat16)
            return carry

        lax.fori_loop(0, n_col, prepare, 0)
    counts_ref[blocks : blocks + listed_ref.shape[0]] = listed_ref[...].astype(jnp.float32)

    row = lax.broadcasted_iota(jnp.int32, (2 * POINT_ROWS, 128), 0)
    fixed = jnp.where((row == 3) | (row == 11), 1.0, jnp.where(row == 5, -FAR, 0.0))
    for u in range(sweeps):
        own_ref[u * 2 * POINT_ROWS : (u + 1) * 2 * POINT_ROWS] = fixed
    turned = jnp.where(lane == 5, 0.0, jnp.where(lane >= 2 * POINT_ROWS, -1.0, 1.0))

    def own(near_column, carry):
        column = share * structures + near_column
        turn = lax.rem(column_here - column + n_col, n_col)
        parts, norm = points(piece_refs[0], turn)
        for place, (high, low) in enumerate(parts):
            for at, value in ((place, high), (place + 8, high), (place + 16, low), (place + 24, low)):
                own_ref[pl.ds(at, sweeps, stride=2 * POINT_ROWS), :] = CONTACT_SLOPE * value
        high, low = split(norm + 0.5 * CONTACT_SHIFT)
        own_ref[pl.ds(4, sweeps, stride=2 * POINT_ROWS), :] = high
        own_ref[pl.ds(20, sweeps, stride=2 * POINT_ROWS), :] = low
        for u in range(sweeps):
            block = u * groups + row_here * n_col + column
            features = jnp.concatenate(
                [
                    own_ref[u * 2 * POINT_ROWS : (u + 1) * 2 * POINT_ROWS],
                    FAR * member(block),
                    jnp.zeros((128 - depth, 128), jnp.float32),
                ],
                axis=0,
            )
            features = jnp.transpose(features)
            slot = near_column * sweeps + u
            first_ref[slot] = features[:, :depth].astype(jnp.bfloat16)
            first_ref[slots + slot] = (features * turned)[:, :depth].astype(jnp.bfloat16)
        return carry

    lax.fori_loop(0, structures, own, 0)

    total_ref[...] = jnp.zeros_like(total_ref)
    spare = 1.0 / (1.0 + jnp.exp(jnp.float32(-CONTACT_SHIFT)))

    def step(turn, carry):
        start = turn * UNIT
        codes = [code_ref[start + t] for t in range(UNIT)]
        sums = sums_ref[pl.ds(0, UNIT, stride=8), :]
        for k in range(1, 8):
            sums = sums + sums_ref[pl.ds(k, UNIT, stride=8), :]
        chance = 64.0 * 128.0 + 0.5 * jnp.sum(sums, axis=1, keepdims=True)
        count = jnp.sum(picks_ref[...], axis=1, keepdims=True)
        chance = jnp.where(diag_ref[...] > 0.5, 0.5 * (chance - 128.0 * spare), chance)
        weight = 1.0 - count / (BACKGROUND + chance / 128.0)
        for t in range(0, UNIT, 2):
            left, right = (second_ref[codes[t + i] & 4095, 0:POINT_ROWS] for i in range(2))
            product = lax.dot_general(
                jnp.concatenate([left, right], axis=0),
                held_ref[t * 128 : (t + 2) * 128],
                (((1,), (1,)), ((), ())),
                preferred_element_type=jnp.float32,
            )
            for i in range(2):
                gain = product[i * POINT_ROWS : (i + 1) * POINT_ROWS, i * 128 : (i + 1) * 128]
                at = pl.multiple_of((codes[t + i] >> 19) * POINT_ROWS, POINT_ROWS)
                total_ref[pl.ds(at, POINT_ROWS), :] += weight[t + i : t + i + 1] * gain
        for t in range(UNIT):
            code = code_ref[start + UNIT + t]
            place = place_ref[start + UNIT + t]
            logit = jnp.dot(
                first_ref[(code >> 12) & 127],
                second_ref[code & 4095],
                preferred_element_type=jnp.float32,
            )
            bend = jnp.tanh(logit)
            sums_ref[t * 8 : (t + 1) * 8] = jnp.sum(bend.reshape(16, 8, 128), axis=0)
            held_ref[t * 128 : (t + 1) * 128] = (1.0 - bend * bend).astype(jnp.bfloat16)
            picked = counts_ref[pl.ds(place >> 7, 1), :]
            picks_ref[t : t + 1] = jnp.where(lane == (place & 127), picked, 0.0)
            band = ((code >> 12) & 127) < slots
            diagonal = band & ((place & 127) == 0)
            diag_ref[t : t + 1] = jnp.full((1, 128), diagonal.astype(jnp.float32))
        return carry

    lax.fori_loop(0, number_ref[0] + 1, step, 0)

    scale = -2.0 * CONTACT_SLOPE / 128.0 / 4.0
    for k in range(structures):
        near_column = lax.rem(place_here + k, structures)
        turn = lax.rem(place_here - near_column + n_col, n_col)
        first = near_column * sweeps * POINT_ROWS
        mass = total_ref[pl.ds(first + 4, sweeps, stride=POINT_ROWS), :]
        for place in range(3):
            high, low = split(piece_refs[0][turn, place])
            pull = (
                total_ref[pl.ds(first + place, sweeps, stride=POINT_ROWS), :]
                + total_ref[pl.ds(first + place + 8, sweeps, stride=POINT_ROWS), :]
            )
            out_refs[k][place] = scale * ((high + low) * mass - pull)


def on_device(n_row, n_col, coords, chrom_lengths, band_counts, inter_pairs, inter_counts):
    structures, _, sweeps, block_size = coords.shape
    band_reach = band_counts.shape[3] - 1
    listed = inter_pairs.shape[1]
    groups = n_row * n_col
    blocks = groups * sweeps
    slots = structures * sweeps
    sizes = (n_row, n_col, structures, sweeps)
    row_here = lax.axis_index("row")
    column_here = lax.axis_index("col")
    member = column_here % structures

    messages = pl.pallas_call(
        functools.partial(pack_kernel, n_col),
        out_shape=[jax.ShapeDtypeStruct((4, sweeps, block_size), jnp.float32)] * n_col,
        in_specs=[VMEM, VMEM],
        out_specs=[VMEM] * n_col,
        name="pack",
    )(coords, band_counts)
    received = [messages[0]]
    for k in range(1, n_col):
        received.append(lax.ppermute(messages[k], "col", [(i, (i + k) % n_col) for i in range(n_col)]))
    own_row = jnp.stack(received)
    pieces = [own_row]
    for k in range(1, n_row):
        pieces.append(lax.ppermute(own_row, "row", [(i, (i + k) % n_row) for i in range(n_row)]))

    chromosomes = chrom_lengths.shape[0]
    numbers = jnp.arange(chromosomes)
    ends = jnp.sum(jnp.where(numbers[None, :] <= numbers[:, None], chrom_lengths[None, :], 0), axis=1)
    starts = ends - chrom_lengths
    slot = jnp.arange(slots)
    block = (
        slot % sweeps * groups
        + row_here * n_col
        + column_here // structures * structures
        + slot // sweeps
    )
    first_bead = block * block_size
    last_bead = first_bead + block_size - 1
    low = jnp.max(jnp.where(starts[None, :] <= first_bead[:, None], starts[None, :], 0), axis=1)
    high = jnp.min(
        jnp.where(ends[None, :] > last_bead[:, None], ends[None, :], blocks * block_size), axis=1
    )
    low = jnp.maximum(low // block_size, block - band_reach)
    high = jnp.minimum(jnp.minimum((high - 1) // block_size, block + band_reach), blocks - 1)
    reach = jnp.stack([low, high]).astype(jnp.int32)
    pairs = jnp.transpose(lax.dynamic_index_in_dim(inter_pairs, member, 0, keepdims=False))
    capacity = slots * (2 * band_reach + 1) + 2 * listed + 4 * UNIT
    code, place, number = pl.pallas_call(
        functools.partial(list_kernel, sizes),
        out_shape=[
            jax.ShapeDtypeStruct((capacity,), jnp.int32),
            jax.ShapeDtypeStruct((capacity,), jnp.int32),
            jax.ShapeDtypeStruct((1,), jnp.int32),
        ],
        in_specs=[SMEM, SMEM],
        out_specs=[SMEM] * 3,
        name="list_tiles",
    )(reach, pairs)

    labels = -(-chromosomes // 16) * 16
    spread = [
        jnp.broadcast_to(jnp.pad(edge, (0, labels - chromosomes))[:, None], (labels, block_size))
        for edge in (starts, ends)
    ]
    counts = lax.dynamic_index_in_dim(inter_counts, member, 0, keepdims=False)
    counts = counts.reshape(listed // block_size, block_size)
    depth = 2 * POINT_ROWS + labels
    gains = pl.pallas_call(
        functools.partial(tile_kernel, sizes),
        out_shape=[jax.ShapeDtypeStruct((3, sweeps, block_size), jnp.float32)] * structures,
        in_specs=[SMEM] * 3 + [VMEM] * (3 + n_row),
        out_specs=[VMEM] * structures,
        scratch_shapes=[
            pltpu.VMEM((blocks, depth, block_size), jnp.bfloat16),
            pltpu.VMEM((2 * slots, block_size, depth), jnp.bfloat16),
            pltpu.VMEM((blocks + listed // block_size, block_size), jnp.float32),
            pltpu.VMEM((sweeps * POINT_ROWS, block_size), jnp.float32),
            pltpu.VMEM((sweeps * 2 * POINT_ROWS, block_size), jnp.float32),
            pltpu.VMEM((UNIT * block_size, block_size), jnp.bfloat16),
            pltpu.VMEM((UNIT * 8, block_size), jnp.float32),
            pltpu.VMEM((UNIT, block_size), jnp.float32),
            pltpu.VMEM((UNIT, block_size), jnp.float32),
            pltpu.VMEM(((slots + 1) * POINT_ROWS, block_size), jnp.float32),
        ],
        compiler_params=pltpu.CompilerParams(vmem_limit_bytes=50 * 1024 * 1024),
        name="tiles",
    )(code, place, number, *spread, counts, *pieces)

    arrived = [gains[0]]
    for k in range(1, structures):
        moves = [
            (base + i, base + (i + k) % structures)
            for base in range(0, n_col, structures)
            for i in range(structures)
        ]
        arrived.append(lax.ppermute(gains[k], "col", moves))
    stacked = jnp.stack(arrived)
    order = (member - jnp.arange(structures)) % structures
    return jnp.take(stacked, order, axis=0)


def solution(mesh):
    placed = (
        P(None, None, None, ("row", "col")),
        P(),
        P(None, None, ("row", "col"), None),
        P(),
        P(),
    )
    return jax.shard_map(
        functools.partial(on_device, mesh.shape["row"], mesh.shape["col"]),
        mesh=mesh,
        in_specs=placed,
        out_specs=P(None, None, None, ("row", "col")),
        check_vma=False,
    )
```

time: 629 us -> 95.2 us (0.15)
  other arithmetic: 407 us -> 1.85 us
  waiting for transfers between devices: 83.4 us -> 5.82 us
  Pallas kernels: 0 us -> 65.4 us
  local copies, waits for them, and re-layouts: 54.1 us -> 3.33 us
  blocking collectives: 44.6 us -> 0 us
  loops' own time: 19.8 us -> 0 us
  starting transfers between devices: 0.09 us -> 17.7 us
  between operations: 13.4 us -> 0.13 us
    reduce_sum x44 -> x1, other arithmetic: 333 us -> 0.11 us  [on_device(): jnp.sum(jnp.where(numbers[None, :] <= numbers[:, None], chrom_lengths[Non...]
    reduce_scatter x2 -> x0, waiting for transfers between devices: 83.4 us -> none  [the longest x1 65 us: on_device(): lax.psum_scatter(column_total.reshape(structures, 3, row_count, sweeps, b...]
    pallas_call x0 -> x3, Pallas kernels: none -> 65.4 us  [the longest x1 32.5 us: on_device(): pl.pallas_call(functools.partial(tile_kernel, sizes), out_shape=[jax.Shap...]
    mul x43 -> x0, other arithmetic: 60.8 us -> none  [the longest x18 51.2 us: pair_tiles(): -2.0 * CONTACT_SLOPE / block_size * (masked * (1.0 - chance))]
    all_gather x3 -> x0, blocking collectives: 44.6 us -> none  [the longest x1 31.9 us: on_device(): column_points = lax.all_gather(local_points, 'row', axis=2, tiled=True)]
    gather x35 -> x1, local copies, waits for them, and re-layouts: 27.5 us -> 0.55 us  [on_device(): return jnp.take(stacked, order, axis=0)]
    another operation x1 -> x0, loops' own time: 19.8 us -> none  [on_device(): lax.scan(sweep, column_total, jnp.arange(sweeps, dtype=jnp.int32))]
    ppermute x0 -> x13, starting transfers between devices: none -> 17.7 us  [the longest x7 11.5 us: on_device(): lax.ppermute(own_row, 'row', [(i, (i + k) % n_row) for i in range(n_row)])]
  transfers between devices with their start and end apart: 2 -> 13, of which waited for: 2 -> 6; matrix products, arithmetic and copies ran while one was open for 0% -> 3% of each run, Pallas kernels for 0% -> 33%
where the time goes in v1:
time: 95.2 us; the launch traced here: 94.2 us
  Pallas kernels  65.4 us (69%)
  starting transfers between devices  17.7 us (19%)
  waiting for transfers between devices  5.82 us (6%)
  local copies, waits for them, and re-layouts  3.33 us (3%)
  other arithmetic  1.85 us (2%)
    pallas_call x1, Pallas kernels, on_device(): pl.pallas_call(functools.partial(tile_kernel, sizes), out_shape=[jax.Shap...  32.5 us
    pallas_call x1, Pallas kernels, on_device(): pl.pallas_call(functools.partial(list_kernel, sizes), out_shape=[jax.Shap...  31.5 us
    ppermute x7, starting transfers between devices, on_device(): lax.ppermute(own_row, 'row', [(i, (i + k) % n_row) for i in range(n_row)])  11.5 us
    ppermute x3, starting transfers between devices, on_device(): lax.ppermute(messages[k], 'col', [(i, (i + k) % n_col) for i in range(n_c...  4.4 us
    ppermute x7, waiting for transfers between devices, on_device(): lax.ppermute(own_row, 'row', [(i, (i + k) % n_row) for i in range(n_row)])  3.84 us
    ppermute x3, waiting for transfers between devices, on_device(): arrived.append(lax.ppermute(gains[k], 'col', moves))  1.98 us
  transfers between devices with their start and end apart: 13, of which 6 were waited for; matrix products, arithmetic and copies ran while one was open for 3% of the time, Pallas kernels for 33%

profile of v1, /device:TPU:0, one launch (start us, length us, event | category | flops | bytes accessed | tf_op | source)
XLA Modules:
  0.0 94.2 jit_solution(8719226816289080493)
XLA Ops:
  0.0 0.0 copy-start
  0.0 1.4 %pack.1 = (f32[4,8,128]{2,1,0:T(8,128)}, f32[4,8,128]{2,1,0:T(8,128)}, f32[4,8,128]{2,1,0:T(8,128)}, f32[4,8,128]{2,1,0:T(8,128)}) custom-call(f32[4,3,8,128]{3,2,1,0:T(8,128)} %coords_ref.1, s32[4,8,1,32]{3,2,1,0:T(1,128)} %counts_ref.1), custom_call_target="tpu_custom_call" | custom-call | tf_op jit(solution)/shard_map/pack/pallas_call | solution.py:257
  1.4 0.5 collective-permute-start
  1.9 2.5 %collective-permute-start.1 = (f32[4,8,128]{2,1,0:T(8,128)}, f32[4,8,128]{2,1,0:T(8,128)S(1)}, u32[]{:S(2)}, u32[]{:S(2)}) collective-permute-start(f32[4,8,128]{2,1,0:T(8,128)} %get-tuple-element.21), channel_id=1, source_target_pairs={{0,2},{1,3},{2,0},{3,1},{4,6},{5,7},{6,4},{7,5},{8,10},{9,11},{10,... | collective-permute-start | bytes 49160 | tf_op jit(solution)/shard_map/ppermute | solution.py:266
  4.4 1.4 %collective-permute-start.2 = (f32[4,8,128]{2,1,0:T(8,128)}, f32[4,8,128]{2,1,0:T(8,128)S(1)}, u32[]{:S(2)}, u32[]{:S(2)}) collective-permute-start(f32[4,8,128]{2,1,0:T(8,128)} %get-tuple-element.22), channel_id=1, source_target_pairs={{0,3},{1,0},{2,1},{3,2},{4,7},{5,4},{6,5},{7,6},{8,11},{9,8},{10,9... | collective-permute-start | bytes 49160 | tf_op jit(solution)/shard_map/ppermute | solution.py:266
  5.9 0.0 copy-start.4
  5.9 0.7 copy-done.4
  6.5 0.1 select_reduce_fusion
  6.6 0.2 select_reduce_fusion.1
  6.8 0.0 copy-done
  6.8 0.6 dynamic-slice_bitcast_fusion.pairs_ref
  7.4 0.7 constant_dynamic-slice_fusion
  8.2 0.0 copy-start.3
  8.2 0.2 select_reduce_fusion.2
  8.4 0.6 pad_add_fusion.reach_ref
  9.0 31.5 %list_tiles.1 = (s32[4096]{0:T(1024)}, s32[4096]{0:T(1024)}, s32[1]{0:T(128)}) custom-call(s32[2,32]{1,0:T(2,128)} %pad_add_fusion.reach_ref, s32[2,1024]{1,0:T(2,128)} %dynamic-slice_bitcast_fusion.pairs_ref), custom_call_target="tpu_custom_call" | custom-call | tf_op jit(solution)/shard_map/list_tiles/pallas_call | solution.py:294
  40.4 0.0 collective-permute-done
  40.5 0.0 collective-permute-done.1
  40.5 0.0 collective-permute-done.2
  40.5 0.0 copy-done.3
  40.5 1.8 %collective-permute-start.3 = (f32[4,4,8,128]{3,2,1,0:T(8,128)S(1)}, f32[4,4,8,128]{3,2,1,0:T(8,128)S(1)}, u32[]{:S(2)}, u32[]{:S(2)}) collective-permute-start(f32[4,4,8,128]{3,2,1,0:T(8,128)S(1)} %pad_maximum_fusion.refs_0_), channel_id=1, source_target_pairs={{0,4},{4,8},{8,12},{12,16},{16,20},{20,24},{24,28},{28,0},{1,5},{5... | collective-permute-start | bytes 196616 | tf_op jit(solution)/shard_map/ppermute | solution.py:270
  42.3 0.2 collective-permute-start.4
  42.5 2.6 %collective-permute-start.5 = (f32[4,4,8,128]{3,2,1,0:T(8,128)S(1)}, f32[4,4,8,128]{3,2,1,0:T(8,128)S(1)}, u32[]{:S(2)}, u32[]{:S(2)}) collective-permute-start(f32[4,4,8,128]{3,2,1,0:T(8,128)S(1)} %pad_maximum_fusion.refs_0_), channel_id=1, source_target_pairs={{0,12},{4,16},{8,20},{12,24},{16,28},{20,0},{24,4},{28,8},{1,13},{... | collective-permute-start | bytes 196616 | tf_op jit(solution)/shard_map/ppermute | solution.py:270
  45.2 2.2 %collective-permute-start.6 = (f32[4,4,8,128]{3,2,1,0:T(8,128)S(1)}, f32[4,4,8,128]{3,2,1,0:T(8,128)S(1)}, u32[]{:S(2)}, u32[]{:S(2)}) collective-permute-start(f32[4,4,8,128]{3,2,1,0:T(8,128)S(1)} %pad_maximum_fusion.refs_0_), channel_id=1, source_target_pairs={{0,16},{4,20},{8,24},{12,28},{16,0},{20,4},{24,8},{28,12},{1,17},{... | collective-permute-start | bytes 196616 | tf_op jit(solution)/shard_map/ppermute | solution.py:270
  47.4 2.2 %collective-permute-start.7 = (f32[4,4,8,128]{3,2,1,0:T(8,128)S(1)}, f32[4,4,8,128]{3,2,1,0:T(8,128)S(1)}, u32[]{:S(2)}, u32[]{:S(2)}) collective-permute-start(f32[4,4,8,128]{3,2,1,0:T(8,128)S(1)} %pad_maximum_fusion.refs_0_), channel_id=1, source_target_pairs={{0,20},{4,24},{8,28},{12,0},{16,4},{20,8},{24,12},{28,16},{1,21},{... | collective-permute-start | bytes 196616 | tf_op jit(solution)/shard_map/ppermute | solution.py:270
  49.5 0.0 collective-permute-done.3.refs_1_
  49.5 2.0 %collective-permute-start.8 = (f32[4,4,8,128]{3,2,1,0:T(8,128)S(1)}, f32[4,4,8,128]{3,2,1,0:T(8,128)S(1)}, u32[]{:S(2)}, u32[]{:S(2)}) collective-permute-start(f32[4,4,8,128]{3,2,1,0:T(8,128)S(1)} %pad_maximum_fusion.refs_0_), channel_id=1, source_target_pairs={{0,24},{4,28},{8,0},{12,4},{16,8},{20,12},{24,16},{28,20},{1,25},{... | collective-permute-start | bytes 196616 | tf_op jit(solution)/shard_map/ppermute | solution.py:270
  51.5 0.0 collective-permute-done.4.refs_2_
  51.5 0.4 collective-permute-start.9
  52.0 0.7 collective-permute-done.5.refs_3_
  52.7 0.0 collective-permute-done.6.refs_4_
  52.7 0.1 collective-permute-done.7.refs_5_
  52.8 1.1 %collective-permute-done.8.refs_6_ = f32[4,4,8,128]{3,2,1,0:T(8,128)S(1)} collective-permute-done((f32[4,4,8,128]{3,2,1,0:T(8,128)S(1)}, f32[4,4,8,128]{3,2,1,0:T(8,128)S(1)}, u32[]{:S(2)}, u32[]{:S(2)}) %collective-permute-start.8) | collective-permute-done | bytes 65568 | tf_op jit(solution)/shard_map/ppermute | solution.py:270
  53.9 1.9 %collective-permute-done.9.refs_7_ = f32[4,4,8,128]{3,2,1,0:T(8,128)S(1)} collective-permute-done((f32[4,4,8,128]{3,2,1,0:T(8,128)S(1)}, f32[4,4,8,128]{3,2,1,0:T(8,128)S(1)}, u32[]{:S(2)}, u32[]{:S(2)}) %collective-permute-start.9) | collective-permute-done | bytes 65568 | tf_op jit(solution)/shard_map/ppermute | solution.py:270
  55.8 0.0 copy-start.2
  55.8 0.1 broadcast_in_dim.64.starts_ref
  55.9 0.0 copy-start.1
  55.9 0.1 broadcast_in_dim.65.ends_ref
  56.0 0.6 copy-done.2
  56.5 0.1 copy-done.1
  56.6 32.5 %tiles.1 = (f32[3,8,128]{2,1,0:T(8,128)S(1)}, f32[3,8,128]{2,1,0:T(8,128)S(1)}, f32[3,8,128]{2,1,0:T(8,128)S(1)}, f32[3,8,128]{2,1,0:T(8,128)S(1)}) custom-call(s32[4096]{0:T(1024)S(1)} %copy-done.1, s32[4096]{0:T(1024)S(1)} %copy-done.2, s32[1]{0:T(128)} %get-tuple-element.18.number_ref, s32[48,128]{1,0:T(8,128)S(1)} %broadcast_in_dim.64.starts_ref, ...), custom_call_target="tpu_custom_call" | custom-call | tf_op jit(solution)/shard_map/tiles/pallas_call | solution.py:314
  89.1 0.1 collective-permute-start.10
  89.2 0.1 collective-permute-start.11
  89.2 1.7 %collective-permute-start.12 = (f32[3,8,128]{2,1,0:T(8,128)S(1)}, f32[3,8,128]{2,1,0:T(8,128)S(1)}, u32[]{:S(2)}, u32[]{:S(2)}) collective-permute-start(f32[3,8,128]{2,1,0:T(8,128)S(1)} %get-tuple-element.26), channel_id=1, source_target_pairs={{0,3},{1,0},{2,1},{3,2},{4,7},{5,4},{6,5},{7,6},{8,11},{9,8},{10,9... | collective-permute-start | bytes 36872 | tf_op jit(solution)/shard_map/ppermute | solution.py:342
  90.9 1.3 %collective-permute-done.10 = f32[3,8,128]{2,1,0:T(8,128)S(1)} collective-permute-done((f32[3,8,128]{2,1,0:T(8,128)S(1)}, f32[3,8,128]{2,1,0:T(8,128)S(1)}, u32[]{:S(2)}, u32[]{:S(2)}) %collective-permute-start.10) | collective-permute-done | bytes 12320 | tf_op jit(solution)/shard_map/ppermute | solution.py:342
  92.3 0.7 collective-permute-done.11
  92.9 0.0 collective-permute-done.12
  92.9 0.6 gather_fusion
  93.5 0.7 broadcast_select_fusion
  (10 shorter events, 0.1 us)
Async XLA Ops:
  0.0 6.8 %copy-start = (s32[4,1024,2]{1,2,0:T(2,128)S(1)}, s32[4,1024,2]{1,2,0:T(2,128)}, u32[]{:S(2)}) copy-start(s32[4,1024,2]{1,2,0:T(2,128)} %param.8) | copy-start | bytes 98308
  1.4 39.0 %collective-permute-start = (f32[4,8,128]{2,1,0:T(8,128)}, f32[4,8,128]{2,1,0:T(8,128)S(1)}, u32[]{:S(2)}, u32[]{:S(2)}) collective-permute-start(f32[4,8,128]{2,1,0:T(8,128)} %get-tuple-element.20), channel_id=1, source_target_pairs={{0,1},{1,2},{2,3},{3,0},{4,5},{5,6},{6,7},{7,4},{8,9},{9,10},{10,1... | collective-permute-start | bytes 49160 | tf_op jit(solution)/shard_map/ppermute | solution.py:266
  1.9 38.6 %collective-permute-start.1 = (f32[4,8,128]{2,1,0:T(8,128)}, f32[4,8,128]{2,1,0:T(8,128)S(1)}, u32[]{:S(2)}, u32[]{:S(2)}) collective-permute-start(f32[4,8,128]{2,1,0:T(8,128)} %get-tuple-element.21), channel_id=1, source_target_pairs={{0,2},{1,3},{2,0},{3,1},{4,6},{5,7},{6,4},{7,5},{8,10},{9,11},{10,... | collective-permute-start | bytes 49160 | tf_op jit(solution)/shard_map/ppermute | solution.py:266
  4.4 36.0 %collective-permute-start.2 = (f32[4,8,128]{2,1,0:T(8,128)}, f32[4,8,128]{2,1,0:T(8,128)S(1)}, u32[]{:S(2)}, u32[]{:S(2)}) collective-permute-start(f32[4,8,128]{2,1,0:T(8,128)} %get-tuple-element.22), channel_id=1, source_target_pairs={{0,3},{1,0},{2,1},{3,2},{4,7},{5,4},{6,5},{7,6},{8,11},{9,8},{10,9... | collective-permute-start | bytes 49160 | tf_op jit(solution)/shard_map/ppermute | solution.py:266
  5.9 0.7 copy-start.4
  8.2 32.3 %copy-start.3 = (f32[4,8,128]{2,1,0:T(8,128)S(1)}, f32[4,8,128]{2,1,0:T(8,128)}, u32[]{:S(2)}) copy-start(f32[4,8,128]{2,1,0:T(8,128)} %get-tuple-element.19) | copy-start | bytes 49156
  40.5 9.0 %collective-permute-start.3 = (f32[4,4,8,128]{3,2,1,0:T(8,128)S(1)}, f32[4,4,8,128]{3,2,1,0:T(8,128)S(1)}, u32[]{:S(2)}, u32[]{:S(2)}) collective-permute-start(f32[4,4,8,128]{3,2,1,0:T(8,128)S(1)} %pad_maximum_fusion.refs_0_), channel_id=1, source_target_pairs={{0,4},{4,8},{8,12},{12,16},{16,20},{20,24},{24,28},{28,0},{1,5},{5... | collective-permute-start | bytes 196616 | tf_op jit(solution)/shard_map/ppermute | solution.py:270
  42.3 9.3 %collective-permute-start.4 = (f32[4,4,8,128]{3,2,1,0:T(8,128)S(1)}, f32[4,4,8,128]{3,2,1,0:T(8,128)S(1)}, u32[]{:S(2)}, u32[]{:S(2)}) collective-permute-start(f32[4,4,8,128]{3,2,1,0:T(8,128)S(1)} %pad_maximum_fusion.refs_0_), channel_id=1, source_target_pairs={{0,8},{4,12},{8,16},{12,20},{16,24},{20,28},{24,0},{28,4},{1,9},{5... | collective-permute-start | bytes 196616 | tf_op jit(solution)/shard_map/ppermute | solution.py:270
  42.5 10.2 %collective-permute-start.5 = (f32[4,4,8,128]{3,2,1,0:T(8,128)S(1)}, f32[4,4,8,128]{3,2,1,0:T(8,128)S(1)}, u32[]{:S(2)}, u32[]{:S(2)}) collective-permute-start(f32[4,4,8,128]{3,2,1,0:T(8,128)S(1)} %pad_maximum_fusion.refs_0_), channel_id=1, source_target_pairs={{0,12},{4,16},{8,20},{12,24},{16,28},{20,0},{24,4},{28,8},{1,13},{... | collective-permute-start | bytes 196616 | tf_op jit(solution)/shard_map/ppermute | solution.py:270
  45.2 7.5 %collective-permute-start.6 = (f32[4,4,8,128]{3,2,1,0:T(8,128)S(1)}, f32[4,4,8,128]{3,2,1,0:T(8,128)S(1)}, u32[]{:S(2)}, u32[]{:S(2)}) collective-permute-start(f32[4,4,8,128]{3,2,1,0:T(8,128)S(1)} %pad_maximum_fusion.refs_0_), channel_id=1, source_target_pairs={{0,16},{4,20},{8,24},{12,28},{16,0},{20,4},{24,8},{28,12},{1,17},{... | collective-permute-start | bytes 196616 | tf_op jit(solution)/shard_map/ppermute | solution.py:270
  47.4 5.5 %collective-permute-start.7 = (f32[4,4,8,128]{3,2,1,0:T(8,128)S(1)}, f32[4,4,8,128]{3,2,1,0:T(8,128)S(1)}, u32[]{:S(2)}, u32[]{:S(2)}) collective-permute-start(f32[4,4,8,128]{3,2,1,0:T(8,128)S(1)} %pad_maximum_fusion.refs_0_), channel_id=1, source_target_pairs={{0,20},{4,24},{8,28},{12,0},{16,4},{20,8},{24,12},{28,16},{1,21},{... | collective-permute-start | bytes 196616 | tf_op jit(solution)/shard_map/ppermute | solution.py:270
  49.5 4.4 %collective-permute-start.8 = (f32[4,4,8,128]{3,2,1,0:T(8,128)S(1)}, f32[4,4,8,128]{3,2,1,0:T(8,128)S(1)}, u32[]{:S(2)}, u32[]{:S(2)}) collective-permute-start(f32[4,4,8,128]{3,2,1,0:T(8,128)S(1)} %pad_maximum_fusion.refs_0_), channel_id=1, source_target_pairs={{0,24},{4,28},{8,0},{12,4},{16,8},{20,12},{24,16},{28,20},{1,25},{... | collective-permute-start | bytes 196616 | tf_op jit(solution)/shard_map/ppermute | solution.py:270
  51.5 4.3 %collective-permute-start.9 = (f32[4,4,8,128]{3,2,1,0:T(8,128)S(1)}, f32[4,4,8,128]{3,2,1,0:T(8,128)S(1)}, u32[]{:S(2)}, u32[]{:S(2)}) collective-permute-start(f32[4,4,8,128]{3,2,1,0:T(8,128)S(1)} %pad_maximum_fusion.refs_0_), channel_id=1, source_target_pairs={{0,28},{4,0},{8,4},{12,8},{16,12},{20,16},{24,20},{28,24},{1,29},{... | collective-permute-start | bytes 196616 | tf_op jit(solution)/shard_map/ppermute | solution.py:270
  55.8 0.7 copy-start.2
  55.9 0.7 copy-start.1
  89.1 3.2 %collective-permute-start.10 = (f32[3,8,128]{2,1,0:T(8,128)S(1)}, f32[3,8,128]{2,1,0:T(8,128)S(1)}, u32[]{:S(2)}, u32[]{:S(2)}) collective-permute-start(f32[3,8,128]{2,1,0:T(8,128)S(1)} %get-tuple-element.24), channel_id=1, source_target_pairs={{0,1},{1,2},{2,3},{3,0},{4,5},{5,6},{6,7},{7,4},{8,9},{9,10},{10,1... | collective-permute-start | bytes 36872 | tf_op jit(solution)/shard_map/ppermute | solution.py:342
  89.2 3.8 %collective-permute-start.11 = (f32[3,8,128]{2,1,0:T(8,128)S(1)}, f32[3,8,128]{2,1,0:T(8,128)S(1)}, u32[]{:S(2)}, u32[]{:S(2)}) collective-permute-start(f32[3,8,128]{2,1,0:T(8,128)S(1)} %get-tuple-element.25), channel_id=1, source_target_pairs={{0,2},{1,3},{2,0},{3,1},{4,6},{5,7},{6,4},{7,5},{8,10},{9,11},{10,... | collective-permute-start | bytes 36872 | tf_op jit(solution)/shard_map/ppermute | solution.py:342
  89.2 3.7 %collective-permute-start.12 = (f32[3,8,128]{2,1,0:T(8,128)S(1)}, f32[3,8,128]{2,1,0:T(8,128)S(1)}, u32[]{:S(2)}, u32[]{:S(2)}) collective-permute-start(f32[3,8,128]{2,1,0:T(8,128)S(1)} %get-tuple-element.26), channel_id=1, source_target_pairs={{0,3},{1,0},{2,1},{3,2},{4,7},{5,4},{6,5},{7,6},{8,11},{9,8},{10,9... | collective-permute-start | bytes 36872 | tf_op jit(solution)/shard_map/ppermute | solution.py:342
